TPU v7x, 768 devices: a whole 4x8x12 slice. The times are simulated.
768 devices in a mesh: band: 48 (over z, y_hi), lev: 4 (over y_lo, core), grp: 4 (over x).
Axes of the slice: x: 4, y: 8 (y_hi: 4, y_lo: 2; y = y_hi * 2 + y_lo), z: 12, core: 2. Of those that a mesh axis runs over, the one named last changes fastest.
Arguments:
- fourier: bfloat16 [3, 8, 2, 2, 4, 288, 1152], P(None, 'lev', None, None, 'grp', 'band'), may hold values from -6 to 6
- legendre: bfloat16 [1152, 2, 576, 4, 288], P('band', None, 'lev', 'grp'), may hold values from -0.1875 to 0.1875
- lat_points: int32 [4, 288], P('grp', 'band'), may hold values from 20 to 4624, as said below
- wave_slots: int32 [1152], replicated, may hold values from 0 to 1151, as said below
- vertical: float32 [8, 8], replicated, may hold values from -2 to 2
Outputs:
- spectral: bfloat16 [1152, 2, 4, 8, 2, 576], P('band', None, None, None, None, ('lev', 'grp'))
Inputs may be any that keep to these rules, and one draw needn't show every extreme that they name: `lat_points`: the values are 20 + 4 i for i = 0 .. 1151, each once (octahedral point counts of the latitude pairs, spread over devices). `wave_slots`: every wavenumber appears once; slots 2 i and 2 i + 1 hold wavenumbers m and 1151 - m.
All inputs are finite; a program needn't handle non-finite values.
Results may differ from a plain program's by a relative error of at most 0.0053.
Values may be sent and summed in bfloat16 or wider, within the bound.
A program may use at most 64 MiB of HBM per device.

v0:
```python
import functools

import jax
import jax.numpy as jnp
from jax import lax
from jax.experimental import pallas as pl
from jax.experimental.pallas import tpu as pltpu
from jax.sharding import PartitionSpec as P

MESH = pl.DeviceIdType.MESH
F32 = jnp.float32
BF16 = jnp.bfloat16

M = 1152
BANDS = 48
SLOTS = 24
LANES = 128
PACK = 32
KROWS = 144
JPAD = 40
COLS = 384


def third(x):
    return (x * 21846) >> 16


def iota(shape, dim):
    return lax.broadcasted_iota(jnp.int32, shape, dim)


def onehot(cond):
    return jnp.where(cond, 1.0, 0.0).astype(BF16)


def roll(x, shift):
    return pltpu.roll(x, shift % LANES, 1)


def dot(a, b):
    return jnp.dot(a, b, preferred_element_type=F32)


def dot_nt(a, b):
    return lax.dot_general(a, b, (((1,), (1,)), ((), ())), preferred_element_type=F32)


def swap_lanes(tiles, bits, lane):
    for bit, shift in bits:
        low = (lane & shift) == 0
        swapped = list(tiles)
        for a in range(len(tiles)):
            if a & bit:
                continue
            x, y = tiles[a], tiles[a | bit]
            swapped[a] = jnp.where(low, x, roll(y, shift))
            swapped[a | bit] = jnp.where(low, roll(x, -shift), y)
        tiles = swapped
    return tiles


def kernel(
    x_ref, leg_hbm, waves_ref, waves_smem, vert_smem, out_ref,
    xp, raw_leg, leg, colperm, expand, staged, band_send, band_recv, gathered, stat, prod, zrows,
    grp_send, grp_recv, m_sel, m_geo_hi, m_geo_lo, leg_tmp,
    leg_sem, bsend_sem, brecv_sem, ysend_sem, yrecv_sem, csend_sem, crecv_sem, fsend_sem, frecv_sem,
    gsend_sem, grecv_sem,
):
    band = lax.axis_index("band")
    lev = lax.axis_index("lev")
    grp = lax.axis_index("grp")
    core_peer = lev + 1 - 2 * (lev % 2)
    y_peer = (lev + 2) % 4
    far = (core_peer + 2) % 4

    barrier = pltpu.get_barrier_semaphore()

    def greet(d, carry):
        pl.semaphore_signal(barrier, inc=1, device_id={"band": (band + d) % BANDS}, device_id_type=MESH)
        return carry

    lax.fori_loop(1, BANDS, greet, 0)
    pl.semaphore_signal(barrier, inc=1, device_id={"lev": core_peer}, device_id_type=MESH)
    pl.semaphore_signal(barrier, inc=1, device_id={"lev": y_peer}, device_id_type=MESH)
    for d in range(1, 4):
        pl.semaphore_signal(barrier, inc=1, device_id={"grp": (grp + d) % 4}, device_id_type=MESH)

    leg_copy = pltpu.make_async_copy(leg_hbm, raw_leg, leg_sem)
    leg_copy.start()

    r = iota((256, 144), 0)
    col = iota((256, 144), 1)
    i, t = r >> 4, r & 15
    f = third(t)
    q = 2 * (t - 3 * f) + (i >> 3)
    src = ((f * 2 + ((i >> 1) & 1)) * 2 + (i & 1)) * 12 + q * 2 + ((i >> 2) & 1)
    place = onehot((t < 9) & (src == col))
    for n in range(0, M, 384):
        xp[:, n : n + 384] = dot(place, x_ref[:, n : n + 384]).astype(BF16)

    lane16 = iota((16, LANES), 1)
    wave_rows = iota((M, LANES), 0)

    def permute(tt, carry):
        for inner in range(3):
            at = pl.multiple_of((tt * 3 + inner) * LANES, LANES)
            table = onehot(wave_rows == waves_ref[:, pl.ds(at, LANES)])
            res = dot(xp[...], table)
            tiles = [res[16 * k : 16 * k + 16] for k in range(16)]
            tiles = swap_lanes(tiles, [(1, 8), (2, 16), (4, 32), (8, 64)], lane16)
            for g in range(16):
                staged[inner * 16 + g] = tiles[g]
        for b in range(16):
            a0, a1, a2 = staged[3 * b], staged[3 * b + 1], staged[3 * b + 2]
            extra = a0[8:16] + pltpu.roll(a1[8:16], 1, 0) + pltpu.roll(a2[8:16], 2, 0)
            packed = jnp.concatenate([a0[:8], a1[:8], a2[:8], extra], axis=0)
            band_send[tt * 16 + b] = packed.astype(BF16)
        return carry

    lax.fori_loop(0, 3, permute, 0)

    pl.semaphore_wait(barrier, BANDS - 1 + 2 + 3)

    def band_copy(d):
        to = (band + d) % BANDS
        return pltpu.make_async_remote_copy(
            src_ref=band_send.at[to], dst_ref=band_recv.at[band], send_sem=bsend_sem, recv_sem=brecv_sem,
            device_id={"band": to}, device_id_type=MESH,
        )

    def start_band(d, carry):
        band_copy(d).start()
        return carry

    lax.fori_loop(1, BANDS, start_band, 0)
    band_recv[band] = band_send[band]

    for k in range(3):
        for f in range(3):
            row = iota((48, 512), 0)
            col = iota((48, 512), 1)
            b = third(row)
            t = row - 3 * b + 3 * f
            expand[(k * 3 + f) * 48 : (k * 3 + f) * 48 + 48, :] = onehot(
                col == b * PACK + jnp.where(t < 8, 8 * k + t, 24 + k)
            )
    row = iota((288, 288), 0)
    col = iota((288, 288), 1)
    half = (col >= KROWS).astype(jnp.int32)
    rest = col - KROWS * half
    b = third(rest)
    colperm[...] = onehot(row == 6 * b + 2 * (rest - 3 * b) + half)

    row = iota((384, COLS), 0)
    col = iota((384, COLS), 1)
    block = third(row >> 4)
    inside = row - 48 * block
    tile, w = col >> 7, col & 127
    u = jnp.where(tile < 2, tile, w >> 6)
    fld = jnp.where(tile < 2, w >> 6, 2)
    lvl = ((w >> 1) & 3) * 2 + ((w >> 4) & 1)
    m_sel[...] = onehot(
        (block == u * 4 + (w & 1) * 2 + ((w >> 5) & 1)) & (inside == fld * 16 + lvl * 2 + ((w >> 3) & 1))
    )
    row = iota((128, LANES), 0)
    w = iota((128, LANES), 1)
    lvl = ((w >> 1) & 3) * 2 + ((w >> 4) & 1)
    same = ((row >> 4) == (w >> 6) * 4 + (w & 1) * 2 + ((w >> 5) & 1)) & ((row & 1) == ((w >> 3) & 1))
    pair = ((row >> 1) & 7) * 8 + lvl
    weight = jnp.zeros((128, LANES), F32)
    for a in range(8):
        for c in range(a, 8):
            weight = jnp.where(pair == a * 8 + c, vert_smem[a, c], weight)
    weight = jnp.where(same, weight, 0.0)
    m_geo_hi[...] = weight.astype(BF16)
    m_geo_lo[...] = (weight - weight.astype(BF16).astype(F32)).astype(BF16)

    leg_copy.wait()
    leg_tmp[288:296, :] = jnp.zeros((8, 288), F32)

    def prepare(s, carry):
        leg_tmp[:288, :] = dot(raw_leg[s].reshape(288, 288), colperm[...])
        for g in range(4):
            leg[s, 80 * g : 80 * g + 80, :] = jnp.concatenate(
                [leg_tmp[36 * g : 36 * g + JPAD, :], leg_tmp[144 + 36 * g : 144 + 36 * g + JPAD, :]], axis=0
            ).astype(BF16)
        return carry

    lax.fori_loop(0, SLOTS, prepare, 0)

    most = pl.ds(0, BANDS - 1)
    pltpu.make_async_remote_copy(
        src_ref=band_send.at[most], dst_ref=band_recv.at[most], send_sem=bsend_sem, recv_sem=brecv_sem,
        device_id={"band": band}, device_id_type=MESH,
    ).wait_recv()
    for c in range(3):
        rows = dot(expand[...], band_recv[16 * c : 16 * c + 16].reshape(512, LANES)).astype(BF16)
        for k in range(3):
            for f in range(3):
                n = (k * 3 + f) * 48
                gathered[lev, k, KROWS * f + 48 * c : KROWS * f + 48 * c + 48, :] = rows[n : n + 48]

    def lev_copy(k, owner, peer, send_sem, recv_sem):
        return pltpu.make_async_remote_copy(
            src_ref=gathered.at[owner, k], dst_ref=gathered.at[owner, k], send_sem=send_sem.at[k],
            recv_sem=recv_sem.at[k], device_id={"lev": peer}, device_id_type=MESH,
        )

    for k in range(3):
        lev_copy(k, lev, y_peer, ysend_sem, yrecv_sem).start()
        lev_copy(k, lev, core_peer, csend_sem, crecv_sem).start()

    lane = iota((16, LANES), 1)
    lane_j = iota((JPAD, LANES), 1)

    def grp_copy(k, d):
        to = (grp + d) % 4
        return pltpu.make_async_remote_copy(
            src_ref=grp_send.at[k, to], dst_ref=grp_recv.at[k, grp], send_sem=gsend_sem.at[k, d - 1],
            recv_sem=grecv_sem.at[k, d - 1], device_id={"grp": to}, device_id_type=MESH,
        )

    def finish(k):
        total = grp_send[k, grp].astype(F32)
        for d in range(1, 4):
            grp_copy(k, d).wait_recv()
            total = total + grp_recv[k, (grp + 4 - d) % 4].astype(F32)
        halves = 36 * (4 * lev + grp) + iota((64, JPAD), 1)
        for h in range(2):
            part = total[JPAD * h : JPAD * h + JPAD]
            hi = part.astype(BF16)
            lo = (part[:, 256:] - hi[:, 256:].astype(F32)).astype(BF16)
            plain = dot_nt(m_sel[...], hi)
            geo = dot_nt(m_geo_hi[...], hi[:, 256:]) + (
                dot_nt(m_geo_hi[...], lo) + dot_nt(m_geo_lo[...], hi[:, 256:])
            )
            for n in range(8):
                s, p = 8 * k + 4 * h + n // 2, n % 2
                wave = waves_smem[band * SLOTS + s]
                values = jnp.concatenate([plain[48 * n : 48 * n + 48], geo[16 * n : 16 * n + 16]], axis=0)
                values = jnp.where(wave + 2 * halves + p <= M - 1, values, 0.0).astype(BF16)
                out_ref[s, p] = values[:, :36]

    for k in range(3):
        lev_copy(k, y_peer, y_peer, ysend_sem, yrecv_sem).wait_recv()
        lev_copy(k, y_peer, core_peer, fsend_sem, frecv_sem).start()
        lev_copy(k, core_peer, core_peer, csend_sem, crecv_sem).wait_recv()
        lev_copy(k, far, core_peer, fsend_sem, frecv_sem).wait_recv()

        def blocks(rb, carry):
            per_field = []
            for f in range(3):
                at = pl.multiple_of(KROWS * f + 16 * rb, 16)
                tiles = [gathered[n, k, pl.ds(at, 16), :].astype(F32) for n in range(4)]
                per_field.append(swap_lanes(tiles, [(2, 4), (1, 2)], lane))
            first = pl.multiple_of(16 * rb, 16)
            second = pl.multiple_of(KROWS + 16 * rb, 16)
            for n in range(4):
                x0, x1, x2 = per_field[0][n], per_field[1][n], per_field[2][n]
                stat[n, pl.ds(first, 16), :LANES] = jnp.where(lane < 64, x0, roll(x1, 64)).astype(BF16)
                stat[n, pl.ds(first, 16), LANES:] = x2.astype(BF16)
                stat[n, pl.ds(second, 16), :LANES] = jnp.where(lane < 64, roll(x0, 64), x1).astype(BF16)
                stat[n, pl.ds(second, 16), LANES:] = roll(x2, 64).astype(BF16)
            return carry

        lax.fori_loop(0, 9, blocks, 0)

        for n in range(4):
            for s in range(2):
                prod[s] = dot(leg[8 * k + 2 * n + s], stat[n])
            for g in range(4):
                for tile in range(2):
                    lanes = slice(LANES * tile, LANES * tile + LANES)
                    even = (lane_j & 1) == 0
                    north = (lane_j & 32) == 0
                    p0 = jnp.where(even, prod[0, 80 * g : 80 * g + 40, lanes], prod[1, 80 * g : 80 * g + 40, lanes])
                    p1 = jnp.where(even, prod[0, 80 * g + 40 : 80 * g + 80, lanes], prod[1, 80 * g + 40 : 80 * g + 80, lanes])
                    zrows[n, 40 * g : 40 * g + 40, lanes] = jnp.where(north, p0 + roll(p0, -32), roll(p1, 32) - p1)
        for g in range(4):
            rows = slice(40 * g, 40 * g + 40)
            halves = []
            for h in range(2):
                last = jnp.where(lane_j < 64, zrows[2 * h, rows, LANES:], roll(zrows[2 * h + 1, rows, LANES:], 64))
                halves.append(jnp.concatenate([zrows[2 * h, rows, :LANES], zrows[2 * h + 1, rows, :LANES], last], axis=1))
            grp_send[k, g] = jnp.concatenate(halves, axis=0).astype(BF16)
        for d in (2, 1, 3):
            grp_copy(k, d).start()
        if k:
            finish(k - 1)
    finish(2)

    pltpu.make_async_remote_copy(
        src_ref=band_send.at[most], dst_ref=band_recv.at[most], send_sem=bsend_sem, recv_sem=brecv_sem,
        device_id={"band": band}, device_id_type=MESH,
    ).wait_send()
    for k in range(3):
        lev_copy(k, lev, y_peer, ysend_sem, yrecv_sem).wait_send()
        lev_copy(k, lev, core_peer, csend_sem, crecv_sem).wait_send()
        lev_copy(k, y_peer, core_peer, fsend_sem, frecv_sem).wait_send()
        for d in range(1, 4):
            grp_copy(k, d).wait_send()


def body(fourier, legendre, lat_points, wave_slots, vertical):
    cutoff = jnp.minimum(M - 1, (lat_points - 1) // 2)[0]
    moved = jnp.transpose(fourier[:, :, :, :, 0], (0, 1, 2, 4, 3, 5))
    kept = iota((1, 1, 1, 6, 1, M), 5) <= cutoff[None, None, None, :, None, None]
    rows = jnp.where(kept, moved, jnp.zeros((), moved.dtype)).reshape(144, M)
    vmem = pl.BlockSpec(memory_space=pltpu.VMEM)
    smem = pl.BlockSpec(memory_space=pltpu.SMEM)
    dma = pltpu.SemaphoreType.DMA
    out = pl.pallas_call(
        kernel,
        out_shape=jax.ShapeDtypeStruct((SLOTS, 2, 64, 36), BF16),
        in_specs=[vmem, pl.BlockSpec(memory_space=pl.ANY), vmem, smem, smem],
        out_specs=vmem,
        scratch_shapes=[
            pltpu.VMEM((256, M), BF16),
            pltpu.VMEM((SLOTS, 2, KROWS, 288), BF16),
            pltpu.VMEM((SLOTS, 320, 288), BF16),
            pltpu.VMEM((288, 288), BF16),
            pltpu.VMEM((432, 512), BF16),
            pltpu.VMEM((48, 16, LANES), F32),
            pltpu.VMEM((BANDS, PACK, LANES), BF16),
            pltpu.VMEM((BANDS, PACK, LANES), BF16),
            pltpu.VMEM((4, 3, 432, LANES), BF16),
            pltpu.VMEM((4, 288, 256), BF16),
            pltpu.VMEM((2, 320, 256), F32),
            pltpu.VMEM((4, 160, 256), F32),
            pltpu.VMEM((3, 4, 80, COLS), BF16),
            pltpu.VMEM((3, 4, 80, COLS), BF16),
            pltpu.VMEM((384, COLS), BF16),
            pltpu.VMEM((128, LANES), BF16),
            pltpu.VMEM((128, LANES), BF16),
            pltpu.VMEM((296, 288), F32),
            dma, dma, dma,
            dma((3,)), dma((3,)), dma((3,)), dma((3,)), dma((3,)), dma((3,)),
            dma((3, 3)), dma((3, 3)),
        ],
        compiler_params=pltpu.CompilerParams(
            collective_id=0, has_side_effects=True, vmem_limit_bytes=48 * 1024 * 1024
        ),
        cost_estimate=pl.CostEstimate(flops=10**9, bytes_accessed=10**7, transcendentals=0),
    )(rows, legendre.reshape(SLOTS, 2, KROWS, 288), wave_slots.reshape(1, M), wave_slots, vertical)
    return out.reshape(SLOTS, 2, 4, 8, 2, 36)


def solution(mesh):
    placed = (
        P(None, "lev", None, None, "grp", "band", None),
        P("band", None, "lev", "grp", None),
        P("grp", "band"),
        P(),
        P(),
    )
    return jax.shard_map(
        body,
        mesh=mesh,
        in_specs=placed,
        out_specs=P("band", None, None, None, None, ("lev", "grp")),
        check_vma=False,
    )
```

profile of v0, /device:TPU:1, one launch (start us, length us, event | category | flops | bytes accessed | tf_op | source)
XLA Modules:
  0.0 67.9 jit_solution(8381150933996920102)
XLA Ops:
  0.0 0.7 minimum_bitcast_fusion
  0.7 0.7 %reshape.34.waves_ref = s32[1,1152]{1,0:T(1,128)S(1)} reshape(s32[1152]{0:T(1024)} %waves_smem.1) | data formatting | bytes 9216 | tf_op jit(solution)/shard_map/reshape | solution.py:344
  1.4 0.1 iota_compare_fusion
  1.4 1.3 %fusion = bf16[3,2,2,6,2,1152]{5,4,3,2,1,0:T(2,128)(2,1)S(1)} fusion(pred[6,1152]{1,0:T(8,128)(4,1)S(1)} %iota_compare_fusion, bf16[3,2,2,2,1,6,1152]{6,3,5,4,2,1,0:T(2,128)(2,1)} %param.5), kind=kLoop, calls=%fused_computation.1 | loop fusion | flops 165888 | bytes 670464 | tf_op jit(solution)/shard_map/jit(_where)/select_n | solution.py:308
  2.7 0.1 reshape.32.x_ref
  2.9 0.0 copy-start
  2.9 0.7 %copy-done = s32[1152]{0:T(1024)S(1)} copy-done((s32[1152]{0:T(1024)S(1)}, s32[1152]{0:T(1024)}, u32[]{:S(2)}) %copy-start) | copy-done | bytes 4632
  3.6 0.0 copy-start.1
  3.6 0.7 %copy-done.1 = f32[8,8]{1,0:T(8,128)S(1)} copy-done((f32[8,8]{1,0:T(8,128)S(1)}, f32[8,8]{1,0:T(8,128)}, u32[]{:S(2)}) %copy-start.1) | copy-done | bytes 280
  4.2 62.7 %shard_map.55 = bf16[24,2,64,36]{3,2,1,0:T(8,128)(2,1)S(1)} custom-call(bf16[144,1152]{1,0:T(8,128)(2,1)S(1)} %reshape.32.x_ref, bf16[24,2,144,288]{3,2,1,0:T(8,128)(2,1)} %bitcast.9, s32[1,1152]{1,0:T(1,128)S(1)} %reshape.34.waves_ref, s32[1152]{0:T(1024)S(1)} %copy-done, f32[8,8]{1,0:T(8,128)S(1)} %copy-done.1), custom_call_target="tpu_custom_call" | custom-call | flops 1000000000 | bytes 10000000 | tf_op jit(solution)/shard_map/pallas_call | solution.py:312
  67.0 0.9 %copy.7 = bf16[24,2,4,8,2,36]{5,4,3,2,1,0:T(2,128)(2,1)} copy(bf16[24,2,4,8,2,36]{5,4,3,2,1,0:T(2,128)(2,1)S(1)} %bitcast.8) | data formatting | bytes 442368
Async XLA Ops:
  2.9 0.7 %copy-start = (s32[1152]{0:T(1024)S(1)}, s32[1152]{0:T(1024)}, u32[]{:S(2)}) copy-start(s32[1152]{0:T(1024)} %waves_smem.1) | copy-start | bytes 13828
  3.6 0.7 %copy-start.1 = (f32[8,8]{1,0:T(8,128)S(1)}, f32[8,8]{1,0:T(8,128)}, u32[]{:S(2)}) copy-start(f32[8,8]{1,0:T(8,128)} %vert_smem.1) | copy-start | bytes 772
where the time goes:
time: 68.1 us; the launch traced here: 67.9 us
  Pallas kernels  62.7 us (92%)
  local copies, waits for them, and re-layouts  3.09 us (5%)
  other arithmetic  2.02 us (3%)
    pallas_call x1, Pallas kernels, body(): pl.pallas_call(kernel, out_shape=jax.ShapeDtypeStruct((SLOTS, 2, 64, 36),...  62.7 us
    unnamed x5, local copies, waits for them, and re-layouts  2.26 us

commit v1 on v0

v1 whole, which is shorter than its diff:
```python
import functools

import jax
import jax.numpy as jnp
from jax import lax
from jax.experimental import pallas as pl
from jax.experimental.pallas import tpu as pltpu
from jax.sharding import PartitionSpec as P

MESH = pl.DeviceIdType.MESH
F32 = jnp.float32
BF16 = jnp.bfloat16

M = 1152
BANDS = 48
SLOTS = 24
LANES = 128
PACK = 32
KROWS = 144
JPAD = 40
COLS = 384


def third(x):
    return (x * 21846) >> 16


def iota(shape, dim):
    return lax.broadcasted_iota(jnp.int32, shape, dim)


def onehot(cond):
    return jnp.where(cond, 1.0, 0.0).astype(BF16)


def roll(x, shift):
    return pltpu.roll(x, shift % LANES, 1)


def dot(a, b):
    return jnp.dot(a, b, preferred_element_type=F32)


def dot_nt(a, b):
    return lax.dot_general(a, b, (((1,), (1,)), ((), ())), preferred_element_type=F32)


def swap_lanes(tiles, bits, lane):
    for bit, shift in bits:
        low = (lane & shift) == 0
        swapped = list(tiles)
        for a in range(len(tiles)):
            if a & bit:
                continue
            x, y = tiles[a], tiles[a | bit]
            swapped[a] = jnp.where(low, x, roll(y, shift))
            swapped[a | bit] = jnp.where(low, roll(x, -shift), y)
        tiles = swapped
    return tiles


def nearest(p):
    odd = p % 2
    return odd * ((p + 1) // 2) - (1 - odd) * (p // 2)


def kernel(
    x_hbm, lat_hbm, waves_hbm, vert_hbm, leg_hbm, out_ref,
    x_ref, lat_ref, waves_ref, vert_ref, xp, raw_leg, leg, colperm, expand, band_send, band_recv, gathered, stat, prod,
    grp_send, grp_recv, m_sel, m_geo_hi, m_geo_lo, leg_tmp, wave_col,
    in_sem, leg_sem, bsend_sem, brecv_sem, ysend_sem, yrecv_sem, csend_sem, crecv_sem, fsend_sem, frecv_sem,
    gsend_sem, grecv_sem,
):
    band = lax.axis_index("band")
    lev = lax.axis_index("lev")
    grp = lax.axis_index("grp")
    z, yh = band // 4, band % 4
    core_peer = lev + 1 - 2 * (lev % 2)
    y_peer = (lev + 2) % 4
    far = (core_peer + 2) % 4

    x_copy = pltpu.make_async_copy(x_hbm, x_ref, in_sem.at[0])
    lat_copy = pltpu.make_async_copy(lat_hbm, lat_ref, in_sem.at[1])
    waves_copy = pltpu.make_async_copy(waves_hbm, waves_ref, in_sem.at[2])
    vert_copy = pltpu.make_async_copy(vert_hbm, vert_ref, in_sem.at[3])
    for copy in (x_copy, lat_copy, waves_copy, vert_copy):
        copy.start()

    barrier = pltpu.get_barrier_semaphore()

    def greet(d, carry):
        pl.semaphore_signal(barrier, inc=1, device_id={"band": (band + d) % BANDS}, device_id_type=MESH)
        return carry

    lax.fori_loop(1, BANDS, greet, 0)
    pl.semaphore_signal(barrier, inc=1, device_id={"lev": core_peer}, device_id_type=MESH)
    pl.semaphore_signal(barrier, inc=1, device_id={"lev": y_peer}, device_id_type=MESH)
    for d in range(1, 4):
        pl.semaphore_signal(barrier, inc=1, device_id={"grp": (grp + d) % 4}, device_id_type=MESH)

    leg_copy = pltpu.make_async_copy(leg_hbm, raw_leg, leg_sem)
    leg_copy.start()

    r = iota((256, 144), 0)
    col = iota((256, 144), 1)
    i, t = r >> 4, r & 15
    f = third(t)
    q = 2 * (t - 3 * f) + (i >> 3)
    src = ((f * 2 + ((i >> 1) & 1)) * 2 + (i & 1)) * 12 + q * 2 + ((i >> 2) & 1)
    place = onehot((t < 9) & (src == col))
    row = iota((384, 384), 0)
    col = iota((384, 384), 1)
    turned = 2 * (((col >> 1) & 3) + 4 - lev & 3) + (col & 1)
    regroup = onehot(row == ((col >> 3) & 15) * 24 + (col >> 7) * 8 + turned)
    pair = iota((144, 384), 0) >> 1
    pair = pair - 6 * third(pair >> 1)
    lat_copy.wait()
    cutoff = jnp.zeros((144, 384), jnp.int32)
    for q in range(6):
        cutoff = jnp.where(pair == q, (lat_ref[0:1, q : q + 1] - 1) >> 1, cutoff)
    x_copy.wait()
    for n in range(0, M, 384):
        lines = x_ref[:, :, n : n + 384].reshape(144, 384)
        kept = jnp.where(iota((144, 384), 1) + n <= cutoff, lines, jnp.zeros((), BF16))
        xp[:, n : n + 384] = dot(place, kept).astype(BF16)

    lane = iota((16, LANES), 1)
    wave_rows = iota((M, LANES), 0)

    def permute(tt, carry):
        parts = []
        line = jnp.concatenate([waves_ref[pl.ds(tt * 3 + n, 1), :] for n in range(3)], axis=1)
        line = jnp.broadcast_to(line, (16, 384))
        digits = jnp.where(iota((16, 384), 0) == 0, line >> 5, line & 31).astype(F32).astype(BF16)
        digits = dot(digits, regroup)
        waves = (32.0 * digits[0:1] + digits[1:2]).astype(jnp.int32)
        for k in range(3):
            res = dot(xp[...], onehot(wave_rows == waves[:, LANES * k : LANES * k + LANES]))
            tiles = [None] * 16
            for n in range(16):
                if n & 4 == 0:
                    north, south = res[16 * n : 16 * n + 16], res[16 * n + 64 : 16 * n + 80]
                    tiles[n], tiles[n | 4] = north + south, north - south
            parts.append(tiles)
        upper = [jnp.concatenate([parts[0][n][:8], parts[1][n][:8]], axis=0).astype(BF16) for n in range(16)]
        lower = []
        for n in range(16):
            extra = parts[0][n][8:] + pltpu.roll(parts[1][n][8:], 1, 0) + pltpu.roll(parts[2][n][8:], 2, 0)
            lower.append(jnp.concatenate([parts[2][n][:8], extra], axis=0).astype(BF16))
        for h, tiles in enumerate((upper, lower)):
            tiles = swap_lanes(tiles, [(1, 8), (2, 16), (4, 32), (8, 64)], lane)
            for g in range(16):
                band_send[tt * 16 + g, 16 * h : 16 * h + 16, :] = tiles[g]
        return carry

    waves_copy.wait()
    lax.fori_loop(0, 3, permute, 0)

    pl.semaphore_wait(barrier, BANDS - 1 + 2 + 3)

    def start_band(c, first):
        def start(t, carry):
            p = 4 * c + t % 4
            to = ((z - nearest(p) + 12) % 12) * 4 + (yh + t // 4) % 4
            pltpu.make_async_remote_copy(
                src_ref=band_send.at[to], dst_ref=band_recv.at[p * 4 + yh], send_sem=bsend_sem,
                recv_sem=brecv_sem.at[c], device_id={"band": to}, device_id_type=MESH,
            ).start()
            return carry

        lax.fori_loop(first, 16, start, 0)

    for c in range(3):
        start_band(c, 1 if c == 0 else 0)
    band_recv[yh] = band_send[band]

    def band_messages(start, count, c):
        part = pl.ds(start, count)
        return pltpu.make_async_remote_copy(
            src_ref=band_send.at[part], dst_ref=band_recv.at[part], send_sem=bsend_sem, recv_sem=brecv_sem.at[c],
            device_id={"band": band}, device_id_type=MESH,
        )

    for k in range(3):
        for f in range(3):
            row = iota((48, 512), 0)
            col = iota((48, 512), 1)
            b = third(row)
            t = row - 3 * b + 3 * f
            expand[(k * 3 + f) * 48 : (k * 3 + f) * 48 + 48, :] = onehot(
                col == b * PACK + jnp.where(t < 8, 8 * k + t, 24 + k)
            )
    row = iota((288, 288), 0)
    col = iota((288, 288), 1)
    half = (col >= KROWS).astype(jnp.int32)
    rest = col - KROWS * half
    b = third(rest)
    p = b >> 2
    away = jnp.where((p & 1) == 1, (p + 1) >> 1, -(p >> 1)) + z
    away = jnp.where(away < 0, away + 12, jnp.where(away >= 12, away - 12, away))
    colperm[...] = onehot(row == 6 * (away * 4 + (b & 3)) + 2 * (rest - 3 * b) + half)

    leg_copy.wait()
    leg_tmp[288:296, :] = jnp.zeros((8, 288), F32)

    def prepare(s, carry):
        leg_tmp[:288, :] = dot(raw_leg[s].reshape(288, 288), colperm[...])
        for g in range(4):
            leg[s, 80 * g : 80 * g + 80, :] = jnp.concatenate(
                [leg_tmp[36 * g : 36 * g + JPAD, :], leg_tmp[144 + 36 * g : 144 + 36 * g + JPAD, :]], axis=0
            ).astype(BF16)
        return carry

    def lev_copy(n, owner, peer, send_sem, recv_sem):
        part = gathered.at[owner, n] if n < 2 else gathered.at[owner, 2, pl.ds(KROWS * (n - 2), KROWS)]
        return pltpu.make_async_remote_copy(
            src_ref=part, dst_ref=part, send_sem=send_sem.at[n], recv_sem=recv_sem.at[n],
            device_id={"lev": peer}, device_id_type=MESH,
        )

    def forward(n):
        lev_copy(n, y_peer, y_peer, ysend_sem, yrecv_sem).wait_recv()
        lev_copy(n, y_peer, core_peer, fsend_sem, frecv_sem).start()

    def send_levels(n):
        lev_copy(n, lev, y_peer, ysend_sem, yrecv_sem).start()
        lev_copy(n, lev, core_peer, csend_sem, crecv_sem).start()

    def levels_here(n):
        lev_copy(n, core_peer, core_peer, csend_sem, crecv_sem).wait_recv()
        lev_copy(n, far, core_peer, fsend_sem, frecv_sem).wait_recv()

    lane48 = iota((48, LANES), 1)

    def sixteen_bands(c):
        band_messages(0, 15 if c == 0 else 16, c).wait_recv()
        rows = dot(expand[...], band_recv[16 * c : 16 * c + 16].reshape(512, LANES)).astype(BF16)
        for k in range(3):
            at = k * KROWS
            x0, x1, x2 = rows[at : at + 48], rows[at + 48 : at + 96], rows[at + 96 : at + 144]
            gathered[lev, c, at : at + 48, :] = jnp.where(lane48 < 64, x0, roll(x1, 64))
            gathered[lev, c, at + 48 : at + 96, :] = jnp.where(lane48 < 64, roll(x0, 64), x1)
            gathered[lev, c, at + 96 : at + 144, :] = x2
            if c == 2:
                send_levels(2 + k)

    lax.fori_loop(0, 8, prepare, 0)
    vert_copy.wait()

    for h in range(2):
        row = iota((384, COLS), 0)
        col = iota((384, COLS), 1)
        block = third(row >> 4)
        inside = row - 48 * block
        tile, w = col >> 7, col & 127
        u = jnp.where(tile < 2, tile, w >> 6)
        fld = jnp.where(tile < 2, w >> 6, 2)
        lvl = ((((w >> 1) & 3) - 2 * h - u) & 3) * 2 + ((w >> 4) & 1)
        m_sel[h] = onehot(
            (block == u * 4 + (w & 1) * 2 + ((w >> 5) & 1)) & (inside == fld * 16 + lvl * 2 + ((w >> 3) & 1))
        )
        row = iota((128, LANES), 0)
        w = iota((128, LANES), 1)
        lvl = ((((w >> 1) & 3) - 2 * h - (w >> 6)) & 3) * 2 + ((w >> 4) & 1)
        same = ((row >> 4) == (w >> 6) * 4 + (w & 1) * 2 + ((w >> 5) & 1)) & ((row & 1) == ((w >> 3) & 1))
        pair = ((row >> 1) & 7) * 8 + lvl
        weight = jnp.zeros((128, LANES), F32)
        for a in range(8):
            for c in range(a, 8):
                weight = jnp.where(pair == a * 8 + c, vert_ref[a : a + 1, c : c + 1], weight)
        weight = jnp.where(same, weight, 0.0)
        m_geo_hi[h] = weight.astype(BF16)
        m_geo_lo[h] = (weight - weight.astype(BF16).astype(F32)).astype(BF16)
    mine = band * SLOTS + iota((SLOTS, LANES), 0)
    owned = jnp.zeros((SLOTS, LANES), F32)
    for n in range(9):
        here = iota((SLOTS, LANES), 1) + LANES * n == mine
        owned = owned + jnp.where(here, waves_ref[n : n + 1, :].astype(F32), 0.0)
    owned = jnp.sum(owned, axis=1, keepdims=True)
    wave_col[...] = jnp.broadcast_to(owned, (SLOTS, LANES)).astype(jnp.int32)

    sixteen_bands(0)
    send_levels(0)
    lax.fori_loop(8, 16, prepare, 0)
    sixteen_bands(1)
    send_levels(1)
    forward(0)
    lax.fori_loop(16, 24, prepare, 0)
    sixteen_bands(2)
    forward(1)
    for n in range(2):
        levels_here(n)

    lane_j = iota((JPAD, LANES), 1)

    def grp_copy(k, d):
        to = (grp + d) % 4
        return pltpu.make_async_remote_copy(
            src_ref=grp_send.at[k, to], dst_ref=grp_recv.at[k, grp], send_sem=gsend_sem.at[k, d - 1],
            recv_sem=grecv_sem.at[k, d - 1], device_id={"grp": to}, device_id_type=MESH,
        )

    def finish(k):
        total = grp_send[k, grp].astype(F32)
        for d in range(1, 4):
            grp_copy(k, d).wait_recv()
            total = total + grp_recv[k, (grp + 4 - d) % 4].astype(F32)
        halves = 36 * (4 * lev + grp) + iota((64, JPAD), 1)
        for h in range(2):
            part = total[JPAD * h : JPAD * h + JPAD]
            hi = part.astype(BF16)
            lo = (part[:, 256:] - hi[:, 256:].astype(F32)).astype(BF16)
            plain = dot_nt(m_sel[h], hi)
            geo = dot_nt(m_geo_hi[h], hi[:, 256:]) + (
                dot_nt(m_geo_hi[h], lo) + dot_nt(m_geo_lo[h], hi[:, 256:])
            )
            for n in range(8):
                s, p = 8 * k + 4 * h + n // 2, n % 2
                values = jnp.concatenate([plain[48 * n : 48 * n + 48], geo[16 * n : 16 * n + 16]], axis=0)
                valid = wave_col[s : s + 1, :JPAD] + 2 * halves + p <= M - 1
                out_ref[s, p] = jnp.where(valid, values, 0.0).astype(BF16)[:, :36]

    group = (lane >> 1) & 3
    forward(2)
    for k in range(3):
        levels_here(2 + k)

        def blocks(rb, carry):
            c, o = rb // 3, rb % 3
            first = pl.multiple_of(16 * rb, 16)
            second = pl.multiple_of(KROWS + 16 * rb, 16)
            per_kind = []
            for f in range(3):
                at = pl.multiple_of(k * KROWS + 48 * f + 16 * o, 16)
                per_kind.append([gathered[n, c, pl.ds(at, 16), :] for n in range(4)])
            for n in range(4):
                picked = []
                for tiles in per_kind:
                    x = tiles[(3 - n) % 4]
                    for a in range(3):
                        x = jnp.where(group == a, tiles[(a - n) % 4], x)
                    picked.append(x)
                stat[n, pl.ds(first, 16), :LANES] = picked[0]
                stat[n, pl.ds(second, 16), :LANES] = picked[1]
                turned = roll(picked[2], 64)
                stat[n, pl.ds(first, 16), LANES:] = turned if n % 2 else picked[2]
                stat[n, pl.ds(second, 16), LANES:] = picked[2] if n % 2 else turned
            return carry

        lax.fori_loop(0, 9, blocks, 0)
        if k < 2:
            forward(3 + k)

        for n in range(8):
            prod[n] = dot(leg[8 * k + n], stat[n // 2])
        even = (lane_j & 1) == 0
        north = (lane_j & 32) == 0
        for g in range(4):
            halves = []
            for h in range(2):
                cols = []
                for n in (2 * h, 2 * h + 1):
                    for tile in range(2):
                        lanes = slice(LANES * tile, LANES * tile + LANES)
                        p0, p1 = slice(80 * g, 80 * g + 40), slice(80 * g + 40, 80 * g + 80)
                        cols.append(
                            jnp.where(
                                north,
                                jnp.where(even, prod[2 * n, p0, lanes], prod[2 * n + 1, p0, lanes]),
                                jnp.where(even, prod[2 * n, p1, lanes], prod[2 * n + 1, p1, lanes]),
                            )
                        )
                halves.append(jnp.concatenate([cols[0], cols[2], jnp.where(lane_j < 64, cols[1], cols[3])], axis=1))
            grp_send[k, g] = jnp.concatenate(halves, axis=0).astype(BF16)
        for d in (2, 1, 3):
            grp_copy(k, d).start()
        if k:
            finish(k - 1)
    finish(2)

    band_messages(0, BANDS - 1, 0).wait_send()
    for n in range(5):
        lev_copy(n, lev, y_peer, ysend_sem, yrecv_sem).wait_send()
        lev_copy(n, lev, core_peer, csend_sem, crecv_sem).wait_send()
        lev_copy(n, y_peer, core_peer, fsend_sem, frecv_sem).wait_send()
    for k in range(3):
        for d in range(1, 4):
            grp_copy(k, d).wait_send()


def body(fourier, legendre, lat_points, wave_slots, vertical):
    moved = jnp.transpose(fourier[:, :, :, :, 0], (0, 1, 2, 4, 3, 5)).reshape(72, 2, M)
    waves = wave_slots.reshape(9, LANES)
    hbm = pl.BlockSpec(memory_space=pltpu.HBM)
    vmem = pl.BlockSpec(memory_space=pltpu.VMEM)
    dma = pltpu.SemaphoreType.DMA
    out = pl.pallas_call(
        kernel,
        out_shape=jax.ShapeDtypeStruct((SLOTS, 2, 64, 36), BF16),
        in_specs=[hbm] * 5,
        out_specs=vmem,
        scratch_shapes=[
            pltpu.VMEM((72, 2, M), BF16),
            pltpu.VMEM((1, 6), jnp.int32),
            pltpu.VMEM((9, LANES), jnp.int32),
            pltpu.VMEM((8, 8), F32),
            pltpu.VMEM((256, M), BF16),
            pltpu.VMEM((SLOTS, 2, KROWS, 288), BF16),
            pltpu.VMEM((SLOTS, 320, 288), BF16),
            pltpu.VMEM((288, 288), BF16),
            pltpu.VMEM((432, 512), BF16),
            pltpu.VMEM((BANDS, PACK, LANES), BF16),
            pltpu.VMEM((BANDS, PACK, LANES), BF16),
            pltpu.VMEM((4, 3, 432, LANES), BF16),
            pltpu.VMEM((4, 288, 256), BF16),
            pltpu.VMEM((8, 320, 256), F32),
            pltpu.VMEM((3, 4, 80, COLS), BF16),
            pltpu.VMEM((3, 4, 80, COLS), BF16),
            pltpu.VMEM((2, 384, COLS), BF16),
            pltpu.VMEM((2, 128, LANES), BF16),
            pltpu.VMEM((2, 128, LANES), BF16),
            pltpu.VMEM((296, 288), F32),
            pltpu.VMEM((SLOTS, LANES), jnp.int32),
            dma((4,)), dma, dma, dma((3,)),
            dma((5,)), dma((5,)), dma((5,)), dma((5,)), dma((5,)), dma((5,)),
            dma((3, 3)), dma((3, 3)),
        ],
        compiler_params=pltpu.CompilerParams(
            collective_id=0, has_side_effects=True, vmem_limit_bytes=48 * 1024 * 1024
        ),
        cost_estimate=pl.CostEstimate(flops=10**9, bytes_accessed=10**7, transcendentals=0),
    )(moved, lat_points, waves, vertical, legendre.reshape(SLOTS, 2, KROWS, 288))
    return out.reshape(SLOTS, 2, 4, 8, 2, 36)


def solution(mesh):
    placed = (
        P(None, "lev", None, None, "grp", "band", None),
        P("band", None, "lev", "grp", None),
        P("grp", "band"),
        P(),
        P(),
    )
    return jax.shard_map(
        body,
        mesh=mesh,
        in_specs=placed,
        out_specs=P("band", None, None, None, None, ("lev", "grp")),
        check_vma=False,
    )
```

time: 68.1 us -> 62.8 us (0.922)
  Pallas kernels: 62.7 us -> 58.6 us
  other arithmetic: 2.02 us -> 0 us
  local copies, waits for them, and re-layouts: 3.09 us -> 3.89 us
    pallas_call x1, Pallas kernels: 62.7 us -> 58.6 us  [body(): pl.pallas_call(kernel, out_shape=jax.ShapeDtypeStruct((SLOTS, 2, 64, 36),...]
    unnamed x5 -> x9, local copies, waits for them, and re-layouts: 2.26 us -> 3.89 us
    select_n x1 -> x0, other arithmetic: 1.28 us -> none  [body(): rows = jnp.where(kept, moved, jnp.zeros((), moved.dtype)).reshape(144, M)]
    reshape x2 -> x0, local copies, waits for them, and re-layouts: 0.83 us -> none  [the longest x1 0.7 us: body(): wave_slots.reshape(1, M)]
    le x2 -> x0, other arithmetic: 0.74 us -> none  [body(): iota((1, 1, 1, 6, 1, M), 5) <= cutoff[None, None, None, :, None, None]]
where the time goes in v1:
time: 62.8 us; the launch traced here: 62.5 us
  Pallas kernels  58.6 us (93%)
  local copies, waits for them, and re-layouts  3.89 us (6%)
    pallas_call x1, Pallas kernels, body(): pl.pallas_call(kernel, out_shape=jax.ShapeDtypeStruct((SLOTS, 2, 64, 36),...  58.6 us
    unnamed x9, local copies, waits for them, and re-layouts  3.89 us

profile of v1, /device:TPU:1, one launch (start us, length us, event | category | flops | bytes accessed | tf_op | source)
XLA Modules:
  0.0 62.5 jit_solution(564725362399470711)
XLA Ops:
  0.0 0.0 copy-start
  0.0 1.0 %copy-done = bf16[3,2,2,2,1,6,1152]{6,3,5,4,2,1,0:T(2,128)(2,1)S(1)} copy-done((bf16[3,2,2,2,1,6,1152]{6,3,5,4,2,1,0:T(2,128)(2,1)S(1)}, bf16[3,2,2,2,1,6,1152]{6,3,5,4,2,1,0:T(2,128)(2,1)}, u32[]{:S(2)}) %copy-start) | copy-done | bytes 331800
  1.0 0.0 copy-start.1
  1.0 0.7 %copy-done.1 = s32[1152]{0:T(1024)S(1)} copy-done((s32[1152]{0:T(1024)S(1)}, s32[1152]{0:T(1024)}, u32[]{:S(2)}) %copy-start.1) | copy-done | bytes 4632
  1.7 0.0 copy-start.2
  1.7 0.7 %copy-done.2 = f32[8,8]{1,0:T(8,128)S(1)} copy-done((f32[8,8]{1,0:T(8,128)S(1)}, f32[8,8]{1,0:T(8,128)}, u32[]{:S(2)}) %copy-start.2) | copy-done | bytes 280
  2.4 0.0 copy-start.3
  2.4 0.7 %copy-done.3 = s32[1,6]{1,0:T(1,128)S(1)} copy-done((s32[1,6]{1,0:T(1,128)S(1)}, s32[1,6]{1,0:T(1,128)}, u32[]{:S(2)}) %copy-start.3) | copy-done | bytes 48
  3.0 58.6 %shard_map.55 = bf16[24,2,64,36]{3,2,1,0:T(8,128)(2,1)S(1)} custom-call(bf16[72,2,1152]{2,1,0:T(2,128)(2,1)S(1)} %bitcast.9, s32[1,6]{1,0:T(1,128)S(1)} %copy-done.3, s32[9,128]{1,0:T(8,128)S(1)} %bitcast.10, f32[8,8]{1,0:T(8,128)S(1)} %copy-done.2, bf16[24,2,144,288]{3,2,1,0:T(8,128)(2,1)} %bitcast.11), custom_call_target="tpu_custom_call" | custom-call | flops 1000000000 | bytes 10000000 | tf_op jit(solution)/shard_map/pallas_call | solution.py:397
  61.6 0.9 %copy.7 = bf16[24,2,4,8,2,36]{5,4,3,2,1,0:T(2,128)(2,1)} copy(bf16[24,2,4,8,2,36]{5,4,3,2,1,0:T(2,128)(2,1)S(1)} %bitcast.8) | data formatting | bytes 442368
Async XLA Ops:
  0.0 1.0 %copy-start = (bf16[3,2,2,2,1,6,1152]{6,3,5,4,2,1,0:T(2,128)(2,1)S(1)}, bf16[3,2,2,2,1,6,1152]{6,3,5,4,2,1,0:T(2,128)(2,1)}, u32[]{:S(2)}) copy-start(bf16[3,2,2,2,1,6,1152]{6,3,5,4,2,1,0:T(2,128)(2,1)} %param.5) | copy-start | bytes 995332
  1.0 0.7 %copy-start.1 = (s32[1152]{0:T(1024)S(1)}, s32[1152]{0:T(1024)}, u32[]{:S(2)}) copy-start(s32[1152]{0:T(1024)} %param.8) | copy-start | bytes 13828
  1.7 0.7 %copy-start.2 = (f32[8,8]{1,0:T(8,128)S(1)}, f32[8,8]{1,0:T(8,128)}, u32[]{:S(2)}) copy-start(f32[8,8]{1,0:T(8,128)} %vert_hbm.1) | copy-start | bytes 772
  2.4 0.7 %copy-start.3 = (s32[1,6]{1,0:T(1,128)S(1)}, s32[1,6]{1,0:T(1,128)}, u32[]{:S(2)}) copy-start(s32[1,6]{1,0:T(1,128)} %lat_hbm.1) | copy-start | bytes 76

commit v2 on v1

--- a/solution.py
+++ b/solution.py
@@ -396,7 +396,7 @@
     dma = pltpu.SemaphoreType.DMA
     out = pl.pallas_call(
         kernel,
-        out_shape=jax.ShapeDtypeStruct((SLOTS, 2, 64, 36), BF16),
+        out_shape=pltpu.VMEM((SLOTS, 2, 64, 36), BF16),
         in_specs=[hbm] * 5,
         out_specs=vmem,
         scratch_shapes=[
@@ -426,7 +426,7 @@
             dma((3, 3)), dma((3, 3)),
         ],
         compiler_params=pltpu.CompilerParams(
-            collective_id=0, has_side_effects=True, vmem_limit_bytes=48 * 1024 * 1024
+            collective_id=0, has_side_effects=True, vmem_limit_bytes=62000000
         ),
         cost_estimate=pl.CostEstimate(flops=10**9, bytes_accessed=10**7, transcendentals=0),
     )(moved, lat_points, waves, vertical, legendre.reshape(SLOTS, 2, KROWS, 288))

time: 62.8 us -> 59.5 us (0.947)
  local copies, waits for them, and re-layouts: 3.89 us -> 0.88 us
    unnamed x9 -> x1, local copies, waits for them, and re-layouts: 3.89 us -> 0.88 us
where the time goes in v2:
time: 59.5 us; the launch traced here: 59.4 us
  Pallas kernels  58.5 us (98%)
  local copies, waits for them, and re-layouts  0.88 us (1%)
    pallas_call x1, Pallas kernels, body(): pl.pallas_call(kernel, out_shape=pltpu.VMEM((SLOTS, 2, 64, 36), BF16), in...  58.5 us

profile of v2, /device:TPU:1, one launch (start us, length us, event | category | flops | bytes accessed | tf_op | source)
XLA Modules:
  0.0 59.4 jit_solution(6294451803016584892)
XLA Ops:
  0.0 58.5 %shard_map.55 = bf16[24,2,64,36]{3,2,1,0:T(8,128)(2,1)S(1)} custom-call(bf16[72,2,1152]{2,1,0:T(2,128)(2,1)} %bitcast.10, s32[1,6]{1,0:T(1,128)} %lat_hbm.1, s32[9,128]{1,0:T(8,128)} %bitcast.11, f32[8,8]{1,0:T(8,128)} %vert_hbm.1, bf16[24,2,144,288]{3,2,1,0:T(8,128)(2,1)} %bitcast.9), custom_call_target="tpu_custom_call" | custom-call | flops 1000000000 | bytes 10000000 | tf_op jit(solution)/shard_map/pallas_call | solution.py:397
  58.5 0.9 %copy.7 = bf16[24,2,4,8,2,36]{5,4,3,2,1,0:T(2,128)(2,1)} copy(bf16[24,2,4,8,2,36]{5,4,3,2,1,0:T(2,128)(2,1)S(1)} %bitcast.8) | data formatting | bytes 442368
